TPU v7x, 512 devices: a whole 4x8x8 slice. The times are simulated.
512 devices in a mesh: chan: 128 (over z, y_hi, x), seg: 4 (over y_lo, core).
Axes of the slice: x: 4, y: 8 (y_hi: 4, y_lo: 2; y = y_hi * 2 + y_lo), z: 8, core: 2. Of those that a mesh axis runs over, the one named last changes fastest.
Arguments:
- strain: float32 [10240, 4096], P('chan', 'seg'), may hold values from -100 to 100, as said below
- alive_flags: int32 [10240, 4], P('chan', 'seg'), may hold values 0 or 1
- plan: int32 [128], replicated, may hold values from 0 to 127, each once
Outputs:
- stacked: bfloat16 [320, 327680], P('seg', 'chan')
Inputs may be any that keep to these rules, and one draw needn't show every extreme that they name: `strain`: the traffic-noise record of each channel; amplitudes vary between channels and over time. `alive_flags`: 1 marks a live channel in a window. `plan`: each of the 128 channel blocks appears once; the first 4 entries name the source blocks in order.
All inputs are finite; a program needn't handle non-finite values. No bound on the sum of `alive_flags` on one device may be relied on, other than what follows from the above.
Results may differ from a plain program's by a relative error of at most 0.011.
Values may be sent and summed in bfloat16 or wider, within the bound.
No kernel may reach another device: no remote copies, remote signals or barrier semaphores. Data moves between devices by JAX's collectives and lax.ppermute only.
A program may use at most 64 MiB of HBM per device.

v0:
```python
import jax
import jax.numpy as jnp
from jax import lax
from jax.sharding import PartitionSpec as P

LAGS = 32
STEPS = 4
SMOOTH = 64


def spread(block, axis, holder):
    block = jnp.where(lax.axis_index(axis) == holder, block, jnp.zeros_like(block))
    return lax.psum(block, axis)


def smoothed_level(records):
    channels, windows, window_len = records.shape
    block_count = window_len // 128
    magnitude = jnp.abs(records).reshape(channels, windows, block_count, 128)
    zero_block = jnp.zeros_like(magnitude[:, :, :1])
    earlier = jnp.concatenate([zero_block, magnitude[:, :, :-1]], axis=2)
    following = jnp.concatenate([magnitude[:, :, 1:], zero_block], axis=2)
    row_index = lax.broadcasted_iota(jnp.int32, (128, 128), 0)
    col_index = lax.broadcasted_iota(jnp.int32, (128, 128), 1)
    inside = (jnp.abs(row_index - col_index) <= SMOOTH).astype(jnp.float32)
    from_earlier = (col_index + 128 - row_index <= SMOOTH).astype(jnp.float32)
    from_following = (row_index + 128 - col_index <= SMOOTH).astype(jnp.float32)
    highest = lax.Precision.HIGHEST
    running = jnp.einsum("cwnu,uv->cwnv", magnitude, inside, precision=highest)
    running = running + jnp.einsum("cwnu,uv->cwnv", earlier, from_earlier, precision=highest)
    running = running + jnp.einsum("cwnu,uv->cwnv", following, from_following, precision=highest)
    position = lax.iota(jnp.int32, window_len)
    samples_in = (
        jnp.minimum(position, SMOOTH) + jnp.minimum(window_len - 1 - position, SMOOTH) + 1
    ).astype(jnp.float32)
    return running.reshape(channels, windows, window_len) / samples_in


def per_device(strain, alive_flags, plan):
    channels = strain.shape[0]
    windows = alive_flags.shape[1]
    window_len = strain.shape[1] // windows
    records = strain.reshape(channels, windows, window_len)
    live_mask = alive_flags.astype(jnp.float32)
    normed = (records / (smoothed_level(records) + 1e-05) * live_mask[:, :, None]).astype(
        jnp.bfloat16
    )
    live_half = live_mask.astype(jnp.bfloat16)
    received = []
    received_live = []
    for source_step in range(STEPS):
        block_data, block_live = (
            spread(normed, "chan", plan[source_step]),
            spread(live_half, "chan", plan[source_step]),
        )
        received.append(block_data)
        received_live.append(block_live)
    sources = jnp.concatenate(received, axis=0)
    source_live = jnp.concatenate(received_live, axis=0).astype(jnp.float32)
    padded = jnp.pad(normed, ((0, 0), (0, 0), (LAGS // 2, LAGS // 2)))
    pieces = []
    for lag_group in range(LAGS // 8):
        shifted = jnp.stack(
            [
                padded[:, :, lag_group * 8 + offset : lag_group * 8 + offset + window_len]
                for offset in range(8)
            ],
            axis=2,
        )
        pieces.append(
            jnp.einsum("swt,rwlt->srl", sources, shifted, preferred_element_type=jnp.float32)
        )
    lagged = jnp.concatenate(pieces, axis=2) / window_len
    source_total = lagged.shape[0]
    counts = jnp.dot(source_live, live_mask.T, preferred_element_type=jnp.float32)
    summed, pairs_sum = (
        lax.psum_scatter(
            lagged.reshape(source_total, channels * LAGS).astype(jnp.bfloat16),
            "seg",
            scatter_dimension=0,
            tiled=True,
        ).astype(jnp.float32),
        lax.psum_scatter(
            counts.astype(jnp.bfloat16), "seg", scatter_dimension=0, tiled=True
        ).astype(jnp.float32),
    )
    kept_rows = summed.shape[0]
    stacked = summed.reshape(kept_rows, channels, LAGS) / jnp.maximum(pairs_sum, 1.0)[:, :, None]
    return stacked.reshape(kept_rows, channels * LAGS).astype(jnp.bfloat16)


def solution(mesh):
    return jax.shard_map(
        per_device,
        mesh=mesh,
        in_specs=(P("chan", "seg"), P("chan", "seg"), P()),
        out_specs=P("seg", "chan"),
        check_vma=False,
    )
```

profile of v0, /device:TPU:1, one launch (start us, length us, event | category | flops | bytes accessed | tf_op | source)
XLA Modules:
  0.0 1437.1 jit_solution(922658526817558228)
XLA Ops:
  7.4 0.7 convert_bitcast_fusion
  8.0 1.0 abs_bitcast_fusion
  9.1 0.3 convolution_bitcast_fusion
  9.5 0.2 copy-done.3
  9.7 0.7 fusion.37
  13.0 0.3 convolution_add_fusion.1
  13.3 0.4 fusion.10
  13.7 0.3 copy-done
  14.1 0.8 select_bitcast_fusion.3
  15.0 335.3 %all-reduce.3 = (bf16[80,1]{0,1:T(2,128)(2,1)S(1)}, bf16[80,1]{0,1:T(2,128)(2,1)S(1)}, bf16[80,1]{0,1:T(2,128)(2,1)S(1)}, bf16[80,1]{0,1:T(2,128)(2,1)S(1)}) all-reduce(bf16[80,1]{0,1:T(2,128)(2,1)S(1)} %get-tuple-element.33, bf16[80,1]{0,1:T(2,128)(2,1)S(1)} %get-tuple-element.34, ...), channel_id=1, replica_groups=mesh['chan'=128,'seg'=4] {'chan'}, use_global_device_ids=true, to_apply=%region_8.9 | all-reduce | flops 320 | bytes 1280 | tf_op jit(solution)/shard_map/psum | solution.py:13
  350.5 0.7 copy.25
  352.2 0.9 bitcast_dynamic-update-slice_fusion.24
  353.8 0.9 bitcast_dynamic-update-slice_fusion.16
  355.1 0.8 bitcast_dynamic-update-slice_fusion.8
  356.0 0.8 bitcast_dynamic-update-slice_fusion.4
  356.8 0.8 bitcast_dynamic-update-slice_fusion.3
  357.5 0.8 bitcast_dynamic-update-slice_fusion.2
  358.3 0.8 bitcast_dynamic-update-slice_fusion.1
  359.1 0.8 bitcast_dynamic-update-slice_fusion
  359.9 969.3 %all-reduce.7.cloned.1.call-done = (bf16[80,1,1024]{2,0,1:T(8,128)(2,1)}, bf16[80,1,1024]{2,0,1:T(8,128)(2,1)}, bf16[80,1,1024]{2,0,1:T(8,128)(2,1)}, bf16[80,1,1024]{2,0,1:T(8,128)(2,1)}) async-done(((bf16[80,1,1024]{2,0,1:T(8,128)(2,1)}, bf16[80,1,1024]{2,0,1:T(8,128)(2,1)}, bf16[80,1,1024]{2,0,1:T(8,128)(2,1)}, bf16[80,1,1024]{2,0,1:T(8,128)(2,1)}), (bf16[80,1,1024]{2,0,1:T(8,128)(2,1)}, ...) | async-done | bytes 655376 | tf_op jit(solution)/shard_map/psum | solution.py:13
  1329.2 2.6 fusion.2
  1331.8 0.9 fusion.4
  1332.7 0.4 copy-done.2
  1333.1 0.9 fusion.6
  1334.0 0.9 fusion.8
  1334.8 0.4 fusion
  1335.2 0.4 copy.17
  1335.7 3.4 copy.23
  1339.1 0.8 copy.26
  1339.9 87.2 %reduce-scatter.7.cloned.1.call-done = bf16[80,2560]{1,0:T(8,128)(2,1)} async-done(((bf16[320,2560]{1,0:T(8,128)(2,1)}), bf16[80,2560]{1,0:T(8,128)(2,1)}) %reduce-scatter.7.cloned.1.call-update) | async-done | bytes 409616
  1427.2 1.3 copy.24
  1428.7 1.0 copy.18
  (50 shorter events, 2.7 us)
Async XLA Ops:
  7.4 1321.8 %all-reduce.7.cloned.1.call-start = ((), (), s32[]{:S(2)}) async-start(), calls=%async_computation.4 | async-start | bytes 1310720 | tf_op jit(solution)/shard_map/psum | solution.py:13
  9.1 0.7 copy-start.3
  13.0 1.0 copy-start
  14.0 1.0 copy-start.4
  14.9 1324.2 %reduce-scatter.9.cloned.1.call-start = ((), (), s32[]{:S(2)}) async-start(), calls=%async_computation.3 | async-start | bytes 102400
  351.3 1075.9 %reduce-scatter.7.cloned.1.call-start = ((), (), s32[]{:S(2)}) async-start(), calls=%async_computation.2 | async-start | bytes 2048000
  354.7 3.7 copy-start.1
  1329.2 2.6 copy-start.5
  1329.2 2.6 copy-start.6
  1329.2 2.6 copy-start.7
  1329.2 2.6 copy-start.8
  1331.8 1.3 copy-start.2
Sparse Core Ops, SparseCore 0:
  15.1 1314.0 all-reduce.6
Sparse Core Ops, SparseCore 1:
  351.4 63.3 reduce-scatter.8
  1339.2 88.0 reduce-scatter.6
where the time goes:
time: 1440 us
  waiting for transfers between devices  1060 us (74%)
  blocking collectives  335 us (23%)
  local copies, waits for them, and re-layouts  17.9 us (1%)
  between operations  17.7 us (1%)
    psum x1, waiting for transfers between devices, spread(): return lax.psum(block, axis)  969 us
    psum x1, blocking collectives, spread(): return lax.psum(block, axis)  335 us
    unnamed x5, waiting for transfers between devices  87.3 us
  transfers between devices with their start and end apart: 3, of which 2 were waited for; matrix products, arithmetic and copies ran while one was open for 1% of the time, Pallas kernels for 0%

commit v1 on v0

v1 whole, which is shorter than its diff:
```python
import jax
import jax.numpy as jnp
from jax import lax
from jax.experimental import pallas as pl
from jax.experimental.pallas import tpu as pltpu
from jax.sharding import Mesh, PartitionSpec as P

CH = 80
WIN = 1024
WINDOWS = 4
LAGS = 32
SMOOTH = 64
FINE = 4
COARSE = LAGS // FINE
PAD = WIN + 128
PIECES = 32
ROWS = 20
PIECE_ROWS = 24
SENT_ROWS = 88
GROUP = 16
GROUPS = CH // GROUP

CHAN = ("z", "yh", "x")
SEG = ("yl", "core")
SCATTER = ("z", "x")
CROSS = ("yh", "yl", "core")

F32 = jnp.float32
BF16 = jnp.bfloat16
VMEM_LIMIT = 48 * 1024 * 1024


def iota(shape, dim):
    return lax.broadcasted_iota(jnp.int32, shape, dim)


def to_column(row, rows):
    width = row.shape[1]
    spread = jnp.broadcast_to(row, (rows, width))
    diagonal = iota((rows, width), 0) == iota((rows, width), 1)
    return jnp.sum(jnp.where(diagonal, spread, 0.0), axis=1, keepdims=True)


def norm_kernel(strain_ref, alive_ref, pieces_ref, own_ref, full, flags):
    live_row = alive_ref[...].astype(F32)
    live_col = to_column(live_row, CH)
    flags[...] = jnp.zeros((8, 128), F32)
    flags[0:1, 0:CH] = live_row
    position = iota((1, WIN), 1)
    samples_in = (
        jnp.minimum(position, SMOOTH) + jnp.minimum(WIN - 1 - position, SMOOTH) + 1
    ).astype(F32)
    for start in range(0, CH, 16):
        x = strain_ref[start : start + 16, :]
        magnitude = jnp.concatenate([jnp.abs(x), jnp.zeros((16, PAD - WIN), F32)], axis=1)
        total = magnitude
        width = 1
        while width < 2 * SMOOTH:
            total = total + pltpu.roll(total, PAD - width, 1)
            width *= 2
        total = pltpu.roll(total, SMOOTH, 1) + pltpu.roll(magnitude, PAD - SMOOTH, 1)
        level = total[:, :WIN] / samples_in
        normed = x / (level + 1e-5) * live_col[start : start + 16]
        full[start : start + 16, :] = normed
        own_ref[start : start + 16, :] = normed.astype(BF16)
    own_ref[CH : CH + 16, :] = jnp.zeros((16, WIN), BF16)
    own_ref[CH : CH + 16, 0:128] = jnp.concatenate(
        [flags[...], jnp.zeros((8, 128), F32)], axis=0
    ).astype(BF16)
    flag_rows = flags[0 : PIECE_ROWS - ROWS, :]
    for piece in range(PIECES):
        h, q = piece // 8, piece % 8
        data = full[h * ROWS : (h + 1) * ROWS, q * 128 : (q + 1) * 128]
        pieces_ref[piece] = jnp.concatenate([data, flag_rows], axis=0).astype(BF16)


def pick_kernel(plan_ref, got_ref, out_ref):
    for k in range(4):
        block = plan_ref[k]
        holder = (block // 16) * 4 + block % 4
        value = got_ref[holder]
        for y in range(4):
            out_ref[y * 4 + k] = value


def fan_kernel(plan_ref, seg_ref, got_ref, out_ref):
    block = plan_ref[seg_ref[0]]
    y = (block // 4) % 4
    pieces = [got_ref[y * 4 + w].astype(F32) for w in range(WINDOWS)]
    rows = [p[:ROWS] for p in pieces] + [p[ROWS : ROWS + 1] for p in pieces]
    rows.append(jnp.zeros((SENT_ROWS - WINDOWS * (ROWS + 1), 128), F32))
    value = jnp.concatenate(rows, axis=0).astype(BF16)
    for piece in range(PIECES):
        out_ref[piece] = value


def correlate_kernel(got_ref, own_ref, out_ref, source, lhs, rhs, total, order):
    row = iota((4 * 128, 4 * 128), 0)
    target = (row % 16) * LAGS + (row // 16 % 8) * FINE + row // 128
    order[...] = (iota((4 * 128, 4 * 128), 1) == target).astype(F32).astype(BF16)
    source[:, :, WIN:] = jnp.zeros((WINDOWS, CH, PAD - WIN), F32)
    for piece in range(PIECES):
        h, q = piece // 8, piece % 8
        value = got_ref[piece].astype(F32)
        for w in range(WINDOWS):
            source[w, h * ROWS : (h + 1) * ROWS, q * 128 : (q + 1) * 128] = value[
                w * ROWS : (w + 1) * ROWS
            ]
    for w in range(WINDOWS):
        block = source[w]
        for a in range(FINE):
            moved = block if a == 0 else pltpu.roll(block, a, 1)
            lhs[a * CH : (a + 1) * CH, :] = moved.astype(BF16)
        for g in range(GROUPS):
            own = own_ref[w, g * GROUP : (g + 1) * GROUP, :].astype(F32)
            own = jnp.concatenate([own, jnp.zeros((GROUP, PAD - WIN), F32)], axis=1)
            for b in range(COARSE):
                shift = (LAGS // 2 - FINE * b) % PAD
                moved = own if shift == 0 else pltpu.roll(own, shift, 1)
                first = g * 128 + b * GROUP
                rhs[first : first + GROUP, :] = moved.astype(BF16)
        partial = lax.dot_general(
            lhs[...], rhs[...], (((1,), (1,)), ((), ())), preferred_element_type=F32
        )
        partial = (partial * (1.0 / WIN)).astype(BF16).astype(F32)
        if w == 0:
            total[...] = partial
        else:
            total[...] += partial
    sent_flags = got_ref[0].astype(F32)[WINDOWS * ROWS : WINDOWS * (ROWS + 1)]
    lane = iota((128, GROUPS * 128), 1)
    channel = (lane // 128) * GROUP + lane % GROUP
    widen = (iota((128, GROUPS * 128), 0) == channel).astype(F32).astype(BF16)
    pairs = jnp.zeros((CH, GROUPS * 128), F32)
    for w in range(WINDOWS):
        own_flags = own_ref[w, CH : CH + 16, 0:128]
        wide = jnp.dot(own_flags, widen, preferred_element_type=F32)[0:1]
        pairs = pairs + to_column(sent_flags[w : w + 1], CH) * wide
    pairs = jnp.maximum(pairs, 1.0)
    scaled = [
        (total[a * CH : (a + 1) * CH, :] / pairs).astype(BF16) for a in range(FINE)
    ]
    for g in range(GROUPS):
        mixed = jnp.concatenate([s[:, g * 128 : (g + 1) * 128] for s in scaled], axis=1)
        out_ref[:, g * 512 : (g + 1) * 512] = jnp.dot(
            mixed, order[...], preferred_element_type=F32
        ).astype(BF16)


def vmem():
    return pl.BlockSpec(memory_space=pltpu.VMEM)


def smem():
    return pl.BlockSpec(memory_space=pltpu.SMEM)


def params():
    return pltpu.CompilerParams(vmem_limit_bytes=VMEM_LIMIT)


def per_device(strain, alive_flags, plan):
    pieces, own = pl.pallas_call(
        norm_kernel,
        out_shape=(
            jax.ShapeDtypeStruct((PIECES, PIECE_ROWS, 128), BF16),
            jax.ShapeDtypeStruct((CH + 16, WIN), BF16),
        ),
        in_specs=[vmem(), vmem()],
        out_specs=(vmem(), vmem()),
        scratch_shapes=[pltpu.VMEM((CH, WIN), F32), pltpu.VMEM((8, 128), F32)],
        compiler_params=params(),
    )(strain, alive_flags.reshape(1, CH))
    segment = (lax.axis_index("yl") * 2 + lax.axis_index("core")).astype(jnp.int32).reshape(1)
    scattered = lax.all_to_all(pieces, SCATTER, 0, 0, tiled=True)
    windows = lax.all_gather(own, SEG, axis=0)
    picked = pl.pallas_call(
        pick_kernel,
        out_shape=jax.ShapeDtypeStruct((16, PIECE_ROWS, 128), BF16),
        in_specs=[smem(), vmem()],
        out_specs=vmem(),
        compiler_params=params(),
    )(plan, scattered)
    crossed = lax.all_to_all(picked, CROSS, 0, 0, tiled=True)
    fanned = pl.pallas_call(
        fan_kernel,
        out_shape=jax.ShapeDtypeStruct((PIECES, SENT_ROWS, 128), BF16),
        in_specs=[smem(), smem(), vmem()],
        out_specs=vmem(),
        compiler_params=params(),
    )(plan, segment, crossed)
    gathered = lax.all_to_all(fanned, SCATTER, 0, 0, tiled=True)
    return pl.pallas_call(
        correlate_kernel,
        out_shape=jax.ShapeDtypeStruct((CH, CH * LAGS), BF16),
        in_specs=[vmem(), vmem()],
        out_specs=vmem(),
        scratch_shapes=[
            pltpu.VMEM((WINDOWS, CH, PAD), F32),
            pltpu.VMEM((FINE * CH, PAD), BF16),
            pltpu.VMEM((GROUPS * 128, PAD), BF16),
            pltpu.VMEM((FINE * CH, GROUPS * 128), F32),
            pltpu.VMEM((512, 512), BF16),
        ],
        compiler_params=params(),
    )(gathered, windows)


def solution(mesh):
    parts = Mesh(mesh.devices.reshape(8, 4, 4, 2, 2), ("z", "yh", "x", "yl", "core"))
    return jax.shard_map(
        per_device,
        mesh=parts,
        in_specs=(P(CHAN, SEG), P(CHAN, SEG), P()),
        out_specs=P(SEG, CHAN),
        check_vma=False,
    )
```

time: 1440 us -> 78.3 us (0.05)
  waiting for transfers between devices: 1060 us -> 21.1 us
  blocking collectives: 335 us -> 32.2 us
  between operations: 17.7 us -> 0.03 us
  local copies, waits for them, and re-layouts: 17.9 us -> 1.63 us
    psum x1 -> x0, waiting for transfers between devices: 969 us -> none  [spread(): return lax.psum(block, axis)]
    psum x1 -> x0, blocking collectives: 335 us -> none  [spread(): return lax.psum(block, axis)]
    unnamed x5 -> x0, waiting for transfers between devices: 87.3 us -> none
    all_to_all x0 -> x1, blocking collectives: none -> 23.4 us  [per_device(): scattered = lax.all_to_all(pieces, SCATTER, 0, 0, tiled=True)]
    all_to_all x0 -> x2, waiting for transfers between devices: none -> 21.1 us  [the longest x1 12.6 us: per_device(): gathered = lax.all_to_all(fanned, SCATTER, 0, 0, tiled=True)]
  transfers between devices with their start and end apart: 3 -> 2, of which waited for: 2 -> 2; matrix products, arithmetic and copies ran while one was open for 1% -> 0% of each run, Pallas kernels for 0% -> 0%
where the time goes in v1:
time: 78.3 us; the launch traced here: 77.9 us
  blocking collectives  32.2 us (41%)
  waiting for transfers between devices  21.1 us (27%)
  starting transfers between devices  13.7 us (17%)
  Pallas kernels  9.24 us (12%)
  local copies, waits for them, and re-layouts  1.63 us (2%)
    all_to_all x1, blocking collectives, per_device(): scattered = lax.all_to_all(pieces, SCATTER, 0, 0, tiled=True)  23.4 us
    all_to_all x1, waiting for transfers between devices, per_device(): gathered = lax.all_to_all(fanned, SCATTER, 0, 0, tiled=True)  12.6 us
    all_to_all x1, starting transfers between devices, per_device(): crossed = lax.all_to_all(picked, CROSS, 0, 0, tiled=True)  9.84 us
    all_gather x1, blocking collectives, per_device(): windows = lax.all_gather(own, SEG, axis=0)  8.72 us
    all_to_all x1, waiting for transfers between devices, per_device(): crossed = lax.all_to_all(picked, CROSS, 0, 0, tiled=True)  8.49 us
    pallas_call x1, Pallas kernels, per_device(): pl.pallas_call(correlate_kernel, out_shape=jax.ShapeDtypeStruct((CH, CH *...  4.89 us
    all_to_all x1, starting transfers between devices, per_device(): gathered = lax.all_to_all(fanned, SCATTER, 0, 0, tiled=True)  3.91 us
    pallas_call x1, Pallas kernels, per_device(): pl.pallas_call(norm_kernel, out_shape=(jax.ShapeDtypeStruct((PIECES, PIEC...  1.66 us
  transfers between devices with their start and end apart: 2, of which 2 were waited for; matrix products, arithmetic and copies ran while one was open for 0% of the time, Pallas kernels for 0%

profile of v1, /device:TPU:1, one launch (start us, length us, event | category | flops | bytes accessed | tf_op | source)
XLA Modules:
  0.0 77.9 jit_solution(5488801595008943267)
XLA Ops:
  0.0 0.0 copy-start.2
  0.0 0.7 copy-done.2
  0.7 0.0 copy-start
  0.7 1.0 %copy-done = f32[80,1024]{1,0:T(8,128)S(1)} copy-done((f32[80,1024]{1,0:T(8,128)S(1)}, f32[80,1024]{1,0:T(8,128)}, u32[]{:S(2)}) %copy-start) | copy-done | bytes 327704
  1.6 1.7 %shard_map.37 = (bf16[32,24,128]{2,1,0:T(8,128)(2,1)S(1)}, bf16[96,1024]{1,0:T(8,128)(2,1)S(1)}) custom-call(f32[80,1024]{1,0:T(8,128)S(1)} %copy-done, s32[1,80]{1,0:T(1,128)S(1)} %bitcast.4), custom_call_target="tpu_custom_call" | custom-call | tf_op jit(solution)/shard_map/pallas_call | solution.py:163
  3.3 0.0 copy-start.1
  3.3 23.4 %all_to_all.15.got_ref = bf16[32,24,128]{2,1,0:T(8,128)(2,1)S(1)} all-to-all(bf16[32,24,128]{2,1,0:T(8,128)(2,1)S(1)} %get-tuple-element.7), channel_id=1, replica_groups=mesh['z'=8,'yh'=4,'x'=4,'yl'=2,'core'=2] {'z','x'}, dimensions={0} | all-to-all | bytes 393216 | tf_op jit(solution)/shard_map/all_to_all | solution.py:175
  26.7 0.0 copy-done.1
  26.7 1.2 %shard_map.38 = bf16[16,24,128]{2,1,0:T(8,128)(2,1)} custom-call(s32[128]{0:T(128)S(1)} %copy-done.1, bf16[32,24,128]{2,1,0:T(8,128)(2,1)S(1)} %all_to_all.15.got_ref), custom_call_target="tpu_custom_call" | custom-call | tf_op jit(solution)/shard_map/pallas_call | solution.py:177
  28.0 9.8 %all-to-all-start.1 = ((bf16[16,24,128]{2,1,0:T(8,128)(2,1)}), bf16[16,24,128]{2,1,0:T(8,128)(2,1)S(1)}, u32[]{:S(2)}, u32[]{:S(2)}) async-start(bf16[16,24,128]{2,1,0:T(8,128)(2,1)} %shard_map.38), calls=%async_computation.1 | async-start | bytes 196608 | tf_op jit(solution)/shard_map/all_to_all | solution.py:184
  37.8 8.5 %all-to-all-done.1.got_ref = bf16[16,24,128]{2,1,0:T(8,128)(2,1)S(1)} async-done(((bf16[16,24,128]{2,1,0:T(8,128)(2,1)}), bf16[16,24,128]{2,1,0:T(8,128)(2,1)S(1)}, u32[]{:S(2)}, u32[]{:S(2)}) %all-to-all-start.1) | async-done | bytes 98336 | tf_op jit(solution)/shard_map/all_to_all | solution.py:184
  46.3 1.5 %shard_map.39 = bf16[32,88,128]{2,1,0:T(8,128)(2,1)} custom-call(s32[128]{0:T(128)S(1)} %copy-done.1, s32[1]{0:T(128)} %bitcast.seg_ref, bf16[16,24,128]{2,1,0:T(8,128)(2,1)S(1)} %all-to-all-done.1.got_ref), custom_call_target="tpu_custom_call" | custom-call | tf_op jit(solution)/shard_map/pallas_call | solution.py:185
  47.8 3.9 %all-to-all-start.2 = ((bf16[32,88,128]{2,1,0:T(8,128)(2,1)}), bf16[32,88,128]{2,1,0:T(8,128)(2,1)S(1)}, u32[]{:S(2)}, u32[]{:S(2)}) async-start(bf16[32,88,128]{2,1,0:T(8,128)(2,1)} %shard_map.39), calls=%async_computation.2 | async-start | bytes 1441792 | tf_op jit(solution)/shard_map/all_to_all | solution.py:192
  51.7 8.7 %all-gather = bf16[384,1024]{1,0:T(8,128)(2,1)S(1)} all-gather(bf16[96,1024]{1,0:T(8,128)(2,1)S(1)} %get-tuple-element.8), channel_id=2, replica_groups=mesh['z'=8,'yh'=4,'x'=4,'yl'=2,'core'=2] {'yl','core'}, dimensions={0}, use_global_device_ids=true | all-gather | bytes 983040 | tf_op jit(solution)/shard_map/all_gather | solution.py:176
  60.4 12.6 %all-to-all-done.2.got_ref = bf16[32,88,128]{2,1,0:T(8,128)(2,1)S(1)} async-done(((bf16[32,88,128]{2,1,0:T(8,128)(2,1)}), bf16[32,88,128]{2,1,0:T(8,128)(2,1)S(1)}, u32[]{:S(2)}, u32[]{:S(2)}) %all-to-all-start.2) | async-done | bytes 720928 | tf_op jit(solution)/shard_map/all_to_all | solution.py:192
  73.1 4.9 %shard_map.40 = bf16[80,2560]{1,0:T(8,128)(2,1)} custom-call(bf16[32,88,128]{2,1,0:T(8,128)(2,1)S(1)} %all-to-all-done.2.got_ref, bf16[4,96,1024]{2,1,0:T(8,128)(2,1)S(1)} %bitcast.3), custom_call_target="tpu_custom_call" | custom-call | tf_op jit(solution)/shard_map/pallas_call | solution.py:193
Async XLA Ops:
  0.0 0.7 copy-start.2
  0.7 1.0 %copy-start = (f32[80,1024]{1,0:T(8,128)S(1)}, f32[80,1024]{1,0:T(8,128)}, u32[]{:S(2)}) copy-start(f32[80,1024]{1,0:T(8,128)} %strain_ref.1) | copy-start | bytes 983044
  3.3 23.5 %copy-start.1 = (s32[128]{0:T(128)S(1)}, s32[128]{0:T(128)}, u32[]{:S(2)}) copy-start(s32[128]{0:T(128)} %plan_ref.3) | copy-start | bytes 1540
  28.0 18.3 %all-to-all-start.1 = ((bf16[16,24,128]{2,1,0:T(8,128)(2,1)}), bf16[16,24,128]{2,1,0:T(8,128)(2,1)S(1)}, u32[]{:S(2)}, u32[]{:S(2)}) async-start(bf16[16,24,128]{2,1,0:T(8,128)(2,1)} %shard_map.38), calls=%async_computation.1 | async-start | bytes 196608 | tf_op jit(solution)/shard_map/all_to_all | solution.py:184
  47.8 25.3 %all-to-all-start.2 = ((bf16[32,88,128]{2,1,0:T(8,128)(2,1)}), bf16[32,88,128]{2,1,0:T(8,128)(2,1)S(1)}, u32[]{:S(2)}, u32[]{:S(2)}) async-start(bf16[32,88,128]{2,1,0:T(8,128)(2,1)} %shard_map.39), calls=%async_computation.2 | async-start | bytes 1441792 | tf_op jit(solution)/shard_map/all_to_all | solution.py:192

commit v2 on v1

--- a/solution.py
+++ b/solution.py
@@ -16,7 +16,7 @@
 PIECES = 32
 ROWS = 20
 PIECE_ROWS = 24
-SENT_ROWS = 88
+SENT_ROWS = WINDOWS * ROWS
 GROUP = 16
 GROUPS = CH // GROUP
 
@@ -27,7 +27,7 @@
 
 F32 = jnp.float32
 BF16 = jnp.bfloat16
-VMEM_LIMIT = 48 * 1024 * 1024
+VMEM_LIMIT = 24 * 1024 * 1024
 
 
 def iota(shape, dim):
@@ -69,7 +69,7 @@
     ).astype(BF16)
     flag_rows = flags[0 : PIECE_ROWS - ROWS, :]
     for piece in range(PIECES):
-        h, q = piece // 8, piece % 8
+        q, h = piece // 4, piece % 4
         data = full[h * ROWS : (h + 1) * ROWS, q * 128 : (q + 1) * 128]
         pieces_ref[piece] = jnp.concatenate([data, flag_rows], axis=0).astype(BF16)
 
@@ -83,24 +83,25 @@
             out_ref[y * 4 + k] = value
 
 
-def fan_kernel(plan_ref, seg_ref, got_ref, out_ref):
-    block = plan_ref[seg_ref[0]]
+def fan_kernel(plan_ref, got_ref, out_ref, flags_ref):
+    pair = lax.axis_index("yl") * 2
+    block = plan_ref[pair + lax.axis_index("core")]
     y = (block // 4) % 4
     pieces = [got_ref[y * 4 + w].astype(F32) for w in range(WINDOWS)]
-    rows = [p[:ROWS] for p in pieces] + [p[ROWS : ROWS + 1] for p in pieces]
-    rows.append(jnp.zeros((SENT_ROWS - WINDOWS * (ROWS + 1), 128), F32))
-    value = jnp.concatenate(rows, axis=0).astype(BF16)
-    for piece in range(PIECES):
-        out_ref[piece] = value
-
-
-def correlate_kernel(got_ref, own_ref, out_ref, source, lhs, rhs, total, order):
+    value = jnp.concatenate([p[:ROWS] for p in pieces], axis=0).astype(BF16)
+    flag_rows = [p[ROWS : ROWS + 1] for p in pieces] + [jnp.zeros((4, 128), F32)]
+    flags_ref[...] = jnp.concatenate(flag_rows, axis=0)
+    for copy in range(out_ref.shape[0]):
+        out_ref[copy] = value
+
+
+def correlate_kernel(got_ref, own_ref, flags_ref, out_ref, source, lhs, rhs, total, order):
     row = iota((4 * 128, 4 * 128), 0)
     target = (row % 16) * LAGS + (row // 16 % 8) * FINE + row // 128
     order[...] = (iota((4 * 128, 4 * 128), 1) == target).astype(F32).astype(BF16)
     source[:, :, WIN:] = jnp.zeros((WINDOWS, CH, PAD - WIN), F32)
     for piece in range(PIECES):
-        h, q = piece // 8, piece % 8
+        q, h = piece // 4, piece % 4
         value = got_ref[piece].astype(F32)
         for w in range(WINDOWS):
             source[w, h * ROWS : (h + 1) * ROWS, q * 128 : (q + 1) * 128] = value[
@@ -127,7 +128,6 @@
             total[...] = partial
         else:
             total[...] += partial
-    sent_flags = got_ref[0].astype(F32)[WINDOWS * ROWS : WINDOWS * (ROWS + 1)]
     lane = iota((128, GROUPS * 128), 1)
     channel = (lane // 128) * GROUP + lane % GROUP
     widen = (iota((128, GROUPS * 128), 0) == channel).astype(F32).astype(BF16)
@@ -135,7 +135,7 @@
     for w in range(WINDOWS):
         own_flags = own_ref[w, CH : CH + 16, 0:128]
         wide = jnp.dot(own_flags, widen, preferred_element_type=F32)[0:1]
-        pairs = pairs + to_column(sent_flags[w : w + 1], CH) * wide
+        pairs = pairs + to_column(flags_ref[w : w + 1, :], CH) * wide
     pairs = jnp.maximum(pairs, 1.0)
     scaled = [
         (total[a * CH : (a + 1) * CH, :] / pairs).astype(BF16) for a in range(FINE)
@@ -171,7 +171,6 @@
         scratch_shapes=[pltpu.VMEM((CH, WIN), F32), pltpu.VMEM((8, 128), F32)],
         compiler_params=params(),
     )(strain, alive_flags.reshape(1, CH))
-    segment = (lax.axis_index("yl") * 2 + lax.axis_index("core")).astype(jnp.int32).reshape(1)
     scattered = lax.all_to_all(pieces, SCATTER, 0, 0, tiled=True)
     windows = lax.all_gather(own, SEG, axis=0)
     picked = pl.pallas_call(
@@ -182,18 +181,21 @@
         compiler_params=params(),
     )(plan, scattered)
     crossed = lax.all_to_all(picked, CROSS, 0, 0, tiled=True)
-    fanned = pl.pallas_call(
+    fanned, source_flags = pl.pallas_call(
         fan_kernel,
-        out_shape=jax.ShapeDtypeStruct((PIECES, SENT_ROWS, 128), BF16),
-        in_specs=[smem(), smem(), vmem()],
-        out_specs=vmem(),
-        compiler_params=params(),
-    )(plan, segment, crossed)
+        out_shape=(
+            jax.ShapeDtypeStruct((PIECES, SENT_ROWS, 128), BF16),
+            jax.ShapeDtypeStruct((8, 128), F32),
+        ),
+        in_specs=[smem(), vmem()],
+        out_specs=(vmem(), vmem()),
+        compiler_params=params(),
+    )(plan, crossed)
     gathered = lax.all_to_all(fanned, SCATTER, 0, 0, tiled=True)
     return pl.pallas_call(
         correlate_kernel,
         out_shape=jax.ShapeDtypeStruct((CH, CH * LAGS), BF16),
-        in_specs=[vmem(), vmem()],
+        in_specs=[vmem()] * 3,
         out_specs=vmem(),
         scratch_shapes=[
             pltpu.VMEM((WINDOWS, CH, PAD), F32),
@@ -203,7 +205,7 @@
             pltpu.VMEM((512, 512), BF16),
         ],
         compiler_params=params(),
-    )(gathered, windows)
+    )(gathered, windows, source_flags)
 
 
 def solution(mesh):

time: 78.3 us -> 76 us (0.971)
  blocking collectives: 32.2 us -> 50.3 us
  waiting for transfers between devices: 21.1 us -> 11.3 us
  starting transfers between devices: 13.7 us -> 3.9 us
    all_to_all x0 -> x1, blocking collectives: none -> 18.1 us  [per_device(): crossed = lax.all_to_all(picked, CROSS, 0, 0, tiled=True)]
    all_to_all x1 -> x0, starting transfers between devices: 9.84 us -> none  [per_device(): crossed = lax.all_to_all(picked, CROSS, 0, 0, tiled=True)]
    all_to_all x1 -> x0, waiting for transfers between devices: 8.49 us -> none  [per_device(): crossed = lax.all_to_all(picked, CROSS, 0, 0, tiled=True)]
    all_to_all x1, waiting for transfers between devices: 12.6 us -> 11.3 us  [per_device(): gathered = lax.all_to_all(fanned, SCATTER, 0, 0, tiled=True)]
  transfers between devices with their start and end apart: 2 -> 1, of which waited for: 2 -> 1; matrix products, arithmetic and copies ran while one was open for 0% -> 0% of each run, Pallas kernels for 0% -> 0%
where the time goes in v2:
time: 76 us; the launch traced here: 75.7 us
  blocking collectives  50.3 us (66%)
  waiting for transfers between devices  11.3 us (15%)
  Pallas kernels  8.59 us (11%)
  starting transfers between devices  3.9 us (5%)
  local copies, waits for them, and re-layouts  1.63 us (2%)
    all_to_all x1, blocking collectives, per_device(): scattered = lax.all_to_all(pieces, SCATTER, 0, 0, tiled=True)  23.4 us
    all_to_all x1, blocking collectives, per_device(): crossed = lax.all_to_all(picked, CROSS, 0, 0, tiled=True)  18.1 us
    all_to_all x1, waiting for transfers between devices, per_device(): gathered = lax.all_to_all(fanned, SCATTER, 0, 0, tiled=True)  11.3 us
    all_gather x1, blocking collectives, per_device(): windows = lax.all_gather(own, SEG, axis=0)  8.72 us
    pallas_call x1, Pallas kernels, per_device(): pl.pallas_call(correlate_kernel, out_shape=jax.ShapeDtypeStruct((CH, CH *...  4.89 us
    all_to_all x1, starting transfers between devices, per_device(): gathered = lax.all_to_all(fanned, SCATTER, 0, 0, tiled=True)  3.9 us
    pallas_call x1, Pallas kernels, per_device(): pl.pallas_call(norm_kernel, out_shape=(jax.ShapeDtypeStruct((PIECES, PIEC...  1.66 us
    unnamed x6, local copies, waits for them, and re-layouts  1.63 us
  transfers between devices with their start and end apart: 1, of which 1 were waited for; matrix products, arithmetic and copies ran while one was open for 0% of the time, Pallas kernels for 0%

profile of v2, /device:TPU:1, one launch (start us, length us, event | category | flops | bytes accessed | tf_op | source)
XLA Modules:
  0.0 75.7 jit_solution(11431127961053789680)
XLA Ops:
  0.0 0.0 copy-start.2
  0.0 0.7 copy-done.2
  0.7 0.0 copy-start
  0.7 1.0 %copy-done = f32[80,1024]{1,0:T(8,128)S(1)} copy-done((f32[80,1024]{1,0:T(8,128)S(1)}, f32[80,1024]{1,0:T(8,128)}, u32[]{:S(2)}) %copy-start) | copy-done | bytes 327704
  1.6 1.7 %shard_map.37 = (bf16[32,24,128]{2,1,0:T(8,128)(2,1)S(1)}, bf16[96,1024]{1,0:T(8,128)(2,1)S(1)}) custom-call(f32[80,1024]{1,0:T(8,128)S(1)} %copy-done, s32[1,80]{1,0:T(1,128)S(1)} %bitcast.3), custom_call_target="tpu_custom_call" | custom-call | tf_op jit(solution)/shard_map/pallas_call | solution.py:163
  3.3 0.0 copy-start.1
  3.3 23.4 %all_to_all.15.got_ref = bf16[32,24,128]{2,1,0:T(8,128)(2,1)S(1)} all-to-all(bf16[32,24,128]{2,1,0:T(8,128)(2,1)S(1)} %get-tuple-element.9), channel_id=1, replica_groups=mesh['z'=8,'yh'=4,'x'=4,'yl'=2,'core'=2] {'z','x'}, dimensions={0} | all-to-all | bytes 393216 | tf_op jit(solution)/shard_map/all_to_all | solution.py:174
  26.7 0.0 copy-done.1
  26.7 0.6 shard_map.38
  27.3 18.1 %all_to_all.16.got_ref = bf16[16,24,128]{2,1,0:T(8,128)(2,1)S(1)} all-to-all(bf16[16,24,128]{2,1,0:T(8,128)(2,1)S(1)} %shard_map.38), channel_id=1, replica_groups=mesh['z'=8,'yh'=4,'x'=4,'yl'=2,'core'=2] {'yh','yl','core'}, dimensions={0} | all-to-all | bytes 196608 | tf_op jit(solution)/shard_map/all_to_all | solution.py:183
  45.5 1.5 %shard_map.39 = (bf16[32,80,128]{2,1,0:T(8,128)(2,1)}, f32[8,128]{1,0:T(8,128)S(1)}) custom-call(s32[128]{0:T(128)S(1)} %copy-done.1, bf16[16,24,128]{2,1,0:T(8,128)(2,1)S(1)} %all_to_all.16.got_ref), custom_call_target="tpu_custom_call" | custom-call | tf_op jit(solution)/shard_map/pallas_call | solution.py:184
  46.9 3.9 %all-to-all-start.2 = ((bf16[32,80,128]{2,1,0:T(8,128)(2,1)}), bf16[32,80,128]{2,1,0:T(8,128)(2,1)S(1)}, u32[]{:S(2)}, u32[]{:S(2)}) async-start(bf16[32,80,128]{2,1,0:T(8,128)(2,1)} %get-tuple-element.10), calls=%async_computation.2 | async-start | bytes 1310720 | tf_op jit(solution)/shard_map/all_to_all | solution.py:194
  50.8 8.7 %all-gather = bf16[384,1024]{1,0:T(8,128)(2,1)S(1)} all-gather(bf16[96,1024]{1,0:T(8,128)(2,1)S(1)} %get-tuple-element.11), channel_id=2, replica_groups=mesh['z'=8,'yh'=4,'x'=4,'yl'=2,'core'=2] {'yl','core'}, dimensions={0}, use_global_device_ids=true | all-gather | bytes 983040 | tf_op jit(solution)/shard_map/all_gather | solution.py:175
  59.5 11.3 %all-to-all-done.2.got_ref = bf16[32,80,128]{2,1,0:T(8,128)(2,1)S(1)} async-done(((bf16[32,80,128]{2,1,0:T(8,128)(2,1)}), bf16[32,80,128]{2,1,0:T(8,128)(2,1)S(1)}, u32[]{:S(2)}, u32[]{:S(2)}) %all-to-all-start.2) | async-done | bytes 655392 | tf_op jit(solution)/shard_map/all_to_all | solution.py:194
  70.8 4.9 %shard_map.40 = bf16[80,2560]{1,0:T(8,128)(2,1)} custom-call(bf16[32,80,128]{2,1,0:T(8,128)(2,1)S(1)} %all-to-all-done.2.got_ref, bf16[4,96,1024]{2,1,0:T(8,128)(2,1)S(1)} %bitcast.2, f32[8,128]{1,0:T(8,128)S(1)} %get-tuple-element.12.flags_ref), custom_call_target="tpu_custom_call" | custom-call | tf_op jit(solution)/shard_map/pallas_call | solution.py:195
Async XLA Ops:
  0.0 0.7 copy-start.2
  0.7 1.0 %copy-start = (f32[80,1024]{1,0:T(8,128)S(1)}, f32[80,1024]{1,0:T(8,128)}, u32[]{:S(2)}) copy-start(f32[80,1024]{1,0:T(8,128)} %strain_ref.1) | copy-start | bytes 983044
  3.3 23.5 %copy-start.1 = (s32[128]{0:T(128)S(1)}, s32[128]{0:T(128)}, u32[]{:S(2)}) copy-start(s32[128]{0:T(128)} %plan_ref.3) | copy-start | bytes 1540
  46.9 23.9 %all-to-all-start.2 = ((bf16[32,80,128]{2,1,0:T(8,128)(2,1)}), bf16[32,80,128]{2,1,0:T(8,128)(2,1)S(1)}, u32[]{:S(2)}, u32[]{:S(2)}) async-start(bf16[32,80,128]{2,1,0:T(8,128)(2,1)} %get-tuple-element.10), calls=%async_computation.2 | async-start | bytes 1310720 | tf_op jit(solution)/shard_map/all_to_all | solution.py:194

commit v3 on v2

--- a/solution.py
+++ b/solution.py
@@ -50,16 +50,24 @@
     samples_in = (
         jnp.minimum(position, SMOOTH) + jnp.minimum(WIN - 1 - position, SMOOTH) + 1
     ).astype(F32)
+    distance = iota((384, 128), 0) - iota((384, 128), 1) - 128
+    band = (jnp.abs(distance) <= SMOOTH).astype(F32).astype(BF16)
+    edge = jnp.zeros((16, 128), BF16)
     for start in range(0, CH, 16):
         x = strain_ref[start : start + 16, :]
-        magnitude = jnp.concatenate([jnp.abs(x), jnp.zeros((16, PAD - WIN), F32)], axis=1)
-        total = magnitude
-        width = 1
-        while width < 2 * SMOOTH:
-            total = total + pltpu.roll(total, PAD - width, 1)
-            width *= 2
-        total = pltpu.roll(total, SMOOTH, 1) + pltpu.roll(magnitude, PAD - SMOOTH, 1)
-        level = total[:, :WIN] / samples_in
+        rest = jnp.abs(x)
+        terms = []
+        for _ in range(3):
+            term = rest.astype(BF16)
+            rest = rest - term.astype(F32)
+            terms.append(jnp.concatenate([edge, term, edge], axis=1))
+        spans = jnp.concatenate(
+            [t[:, b * 128 : b * 128 + 384] for t in terms for b in range(8)], axis=0
+        )
+        sums = jnp.dot(spans, band, preferred_element_type=F32)
+        sums = sums[0:128] + sums[128:256] + sums[256:384]
+        total = jnp.concatenate([sums[b * 16 : (b + 1) * 16] for b in range(8)], axis=1)
+        level = total / samples_in
         normed = x / (level + 1e-5) * live_col[start : start + 16]
         full[start : start + 16, :] = normed
         own_ref[start : start + 16, :] = normed.astype(BF16)
@@ -95,10 +103,30 @@
         out_ref[copy] = value
 
 
-def correlate_kernel(got_ref, own_ref, flags_ref, out_ref, source, lhs, rhs, total, order):
+def correlate_kernel(
+    got_ref, own_ref, flags_ref, out_hbm, source, lhs, rhs, total, order, out_ref, sems
+):
     row = iota((4 * 128, 4 * 128), 0)
     target = (row % 16) * LAGS + (row // 16 % 8) * FINE + row // 128
     order[...] = (iota((4 * 128, 4 * 128), 1) == target).astype(F32).astype(BF16)
+    for w in range(WINDOWS):
+        for g in range(GROUPS):
+            own = own_ref[w, g * GROUP : (g + 1) * GROUP, :].astype(F32)
+            own = jnp.concatenate([own, jnp.zeros((GROUP, PAD - WIN), F32)], axis=1)
+            for b in range(COARSE):
+                shift = (LAGS // 2 - FINE * b) % PAD
+                moved = own if shift == 0 else pltpu.roll(own, shift, 1)
+                first = g * 128 + b * GROUP
+                rhs[w, first : first + GROUP, :] = moved.astype(BF16)
+    lane = iota((128, GROUPS * 128), 1)
+    channel = (lane // 128) * GROUP + lane % GROUP
+    widen = (iota((128, GROUPS * 128), 0) == channel).astype(F32).astype(BF16)
+    pairs = jnp.zeros((CH, GROUPS * 128), F32)
+    for w in range(WINDOWS):
+        own_flags = own_ref[w, CH : CH + 16, 0:128]
+        wide = jnp.dot(own_flags, widen, preferred_element_type=F32)[0:1]
+        pairs = pairs + to_column(flags_ref[w : w + 1, :], CH) * wide
+    pairs = jnp.maximum(pairs, 1.0)
     source[:, :, WIN:] = jnp.zeros((WINDOWS, CH, PAD - WIN), F32)
     for piece in range(PIECES):
         q, h = piece // 4, piece % 4
@@ -111,40 +139,33 @@
         block = source[w]
         for a in range(FINE):
             moved = block if a == 0 else pltpu.roll(block, a, 1)
-            lhs[a * CH : (a + 1) * CH, :] = moved.astype(BF16)
-        for g in range(GROUPS):
-            own = own_ref[w, g * GROUP : (g + 1) * GROUP, :].astype(F32)
-            own = jnp.concatenate([own, jnp.zeros((GROUP, PAD - WIN), F32)], axis=1)
-            for b in range(COARSE):
-                shift = (LAGS // 2 - FINE * b) % PAD
-                moved = own if shift == 0 else pltpu.roll(own, shift, 1)
-                first = g * 128 + b * GROUP
-                rhs[first : first + GROUP, :] = moved.astype(BF16)
+            lhs[w, a * CH : (a + 1) * CH, :] = moved.astype(BF16)
+    for w in range(WINDOWS):
         partial = lax.dot_general(
-            lhs[...], rhs[...], (((1,), (1,)), ((), ())), preferred_element_type=F32
+            lhs[w], rhs[w], (((1,), (1,)), ((), ())), preferred_element_type=F32
         )
         partial = (partial * (1.0 / WIN)).astype(BF16).astype(F32)
         if w == 0:
             total[...] = partial
         else:
             total[...] += partial
-    lane = iota((128, GROUPS * 128), 1)
-    channel = (lane // 128) * GROUP + lane % GROUP
-    widen = (iota((128, GROUPS * 128), 0) == channel).astype(F32).astype(BF16)
-    pairs = jnp.zeros((CH, GROUPS * 128), F32)
-    for w in range(WINDOWS):
-        own_flags = own_ref[w, CH : CH + 16, 0:128]
-        wide = jnp.dot(own_flags, widen, preferred_element_type=F32)[0:1]
-        pairs = pairs + to_column(flags_ref[w : w + 1, :], CH) * wide
-    pairs = jnp.maximum(pairs, 1.0)
     scaled = [
         (total[a * CH : (a + 1) * CH, :] / pairs).astype(BF16) for a in range(FINE)
     ]
+    copies = []
     for g in range(GROUPS):
         mixed = jnp.concatenate([s[:, g * 128 : (g + 1) * 128] for s in scaled], axis=1)
-        out_ref[:, g * 512 : (g + 1) * 512] = jnp.dot(
+        columns = pl.ds(g * 512, 512)
+        out_ref[:, columns] = jnp.dot(
             mixed, order[...], preferred_element_type=F32
         ).astype(BF16)
+        copy = pltpu.make_async_copy(
+            out_ref.at[:, columns], out_hbm.at[:, columns], sems.at[g]
+        )
+        copy.start()
+        copies.append(copy)
+    for copy in copies:
+        copy.wait()
 
 
 def vmem():
@@ -196,15 +217,18 @@
         correlate_kernel,
         out_shape=jax.ShapeDtypeStruct((CH, CH * LAGS), BF16),
         in_specs=[vmem()] * 3,
-        out_specs=vmem(),
+        out_specs=pl.BlockSpec(memory_space=pl.ANY),
         scratch_shapes=[
             pltpu.VMEM((WINDOWS, CH, PAD), F32),
-            pltpu.VMEM((FINE * CH, PAD), BF16),
-            pltpu.VMEM((GROUPS * 128, PAD), BF16),
+            pltpu.VMEM((WINDOWS, FINE * CH, PAD), BF16),
+            pltpu.VMEM((WINDOWS, GROUPS * 128, PAD), BF16),
             pltpu.VMEM((FINE * CH, GROUPS * 128), F32),
             pltpu.VMEM((512, 512), BF16),
+            pltpu.VMEM((CH, CH * LAGS), BF16),
+            pltpu.SemaphoreType.DMA((GROUPS,)),
         ],
         compiler_params=params(),
+        cost_estimate=pl.CostEstimate(flops=3400000000, bytes_accessed=2000000, transcendentals=0),
     )(gathered, windows, source_flags)
 
 

time: 76 us -> 74.5 us (0.980)
  Pallas kernels: 8.59 us -> 7.04 us
    pallas_call x1, Pallas kernels: 1.66 us -> 0.57 us  [per_device(): pl.pallas_call(norm_kernel, out_shape=(jax.ShapeDtypeStruct((PIECES, PIEC...]
where the time goes in v3:
time: 74.5 us; the launch traced here: 74.2 us
  blocking collectives  50.3 us (68%)
  waiting for transfers between devices  11.3 us (15%)
  Pallas kernels  7.04 us (9%)
  starting transfers between devices  3.9 us (5%)
  local copies, waits for them, and re-layouts  1.63 us (2%)
    all_to_all x1, blocking collectives, per_device(): scattered = lax.all_to_all(pieces, SCATTER, 0, 0, tiled=True)  23.4 us
    all_to_all x1, blocking collectives, per_device(): crossed = lax.all_to_all(picked, CROSS, 0, 0, tiled=True)  18.1 us
    all_to_all x1, waiting for transfers between devices, per_device(): gathered = lax.all_to_all(fanned, SCATTER, 0, 0, tiled=True)  11.3 us
    all_gather x1, blocking collectives, per_device(): windows = lax.all_gather(own, SEG, axis=0)  8.72 us
    pallas_call x1, Pallas kernels, per_device(): pl.pallas_call(correlate_kernel, out_shape=jax.ShapeDtypeStruct((CH, CH *...  4.43 us
    all_to_all x1, starting transfers between devices, per_device(): gathered = lax.all_to_all(fanned, SCATTER, 0, 0, tiled=True)  3.9 us
    unnamed x6, local copies, waits for them, and re-layouts  1.63 us
  transfers between devices with their start and end apart: 1, of which 1 were waited for; matrix products, arithmetic and copies ran while one was open for 0% of the time, Pallas kernels for 0%

profile of v3, /device:TPU:1, one launch (start us, length us, event | category | flops | bytes accessed | tf_op | source)
XLA Modules:
  0.0 74.2 jit_solution(16884651065799298908)
XLA Ops:
  0.0 0.0 copy-start.2
  0.0 0.7 copy-done.2
  0.7 0.0 copy-start
  0.7 1.0 %copy-done = f32[80,1024]{1,0:T(8,128)S(1)} copy-done((f32[80,1024]{1,0:T(8,128)S(1)}, f32[80,1024]{1,0:T(8,128)}, u32[]{:S(2)}) %copy-start) | copy-done | bytes 327704
  1.6 0.6 shard_map.37
  2.2 0.0 copy-start.1
  2.2 23.4 %all_to_all.15.got_ref = bf16[32,24,128]{2,1,0:T(8,128)(2,1)S(1)} all-to-all(bf16[32,24,128]{2,1,0:T(8,128)(2,1)S(1)} %get-tuple-element.9), channel_id=1, replica_groups=mesh['z'=8,'yh'=4,'x'=4,'yl'=2,'core'=2] {'z','x'}, dimensions={0} | all-to-all | bytes 393216 | tf_op jit(solution)/shard_map/all_to_all | solution.py:195
  25.7 0.0 copy-done.1
  25.7 0.6 shard_map.38
  26.2 18.1 %all_to_all.16.got_ref = bf16[16,24,128]{2,1,0:T(8,128)(2,1)S(1)} all-to-all(bf16[16,24,128]{2,1,0:T(8,128)(2,1)S(1)} %shard_map.38), channel_id=1, replica_groups=mesh['z'=8,'yh'=4,'x'=4,'yl'=2,'core'=2] {'yh','yl','core'}, dimensions={0} | all-to-all | bytes 196608 | tf_op jit(solution)/shard_map/all_to_all | solution.py:204
  44.4 1.5 %shard_map.39 = (bf16[32,80,128]{2,1,0:T(8,128)(2,1)}, f32[8,128]{1,0:T(8,128)S(1)}) custom-call(s32[128]{0:T(128)S(1)} %copy-done.1, bf16[16,24,128]{2,1,0:T(8,128)(2,1)S(1)} %all_to_all.16.got_ref), custom_call_target="tpu_custom_call" | custom-call | tf_op jit(solution)/shard_map/pallas_call | solution.py:205
  45.8 3.9 %all-to-all-start.2 = ((bf16[32,80,128]{2,1,0:T(8,128)(2,1)}), bf16[32,80,128]{2,1,0:T(8,128)(2,1)S(1)}, u32[]{:S(2)}, u32[]{:S(2)}) async-start(bf16[32,80,128]{2,1,0:T(8,128)(2,1)} %get-tuple-element.10), calls=%async_computation.2 | async-start | bytes 1310720 | tf_op jit(solution)/shard_map/all_to_all | solution.py:215
  49.7 8.7 %all-gather = bf16[384,1024]{1,0:T(8,128)(2,1)S(1)} all-gather(bf16[96,1024]{1,0:T(8,128)(2,1)S(1)} %get-tuple-element.11), channel_id=2, replica_groups=mesh['z'=8,'yh'=4,'x'=4,'yl'=2,'core'=2] {'yl','core'}, dimensions={0}, use_global_device_ids=true | all-gather | bytes 983040 | tf_op jit(solution)/shard_map/all_gather | solution.py:196
  58.5 11.3 %all-to-all-done.2.got_ref = bf16[32,80,128]{2,1,0:T(8,128)(2,1)S(1)} async-done(((bf16[32,80,128]{2,1,0:T(8,128)(2,1)}), bf16[32,80,128]{2,1,0:T(8,128)(2,1)S(1)}, u32[]{:S(2)}, u32[]{:S(2)}) %all-to-all-start.2) | async-done | bytes 655392 | tf_op jit(solution)/shard_map/all_to_all | solution.py:215
  69.8 4.4 %shard_map.40 = bf16[80,2560]{1,0:T(8,128)(2,1)} custom-call(bf16[32,80,128]{2,1,0:T(8,128)(2,1)S(1)} %all-to-all-done.2.got_ref, bf16[4,96,1024]{2,1,0:T(8,128)(2,1)S(1)} %bitcast.2, f32[8,128]{1,0:T(8,128)S(1)} %get-tuple-element.12.flags_ref), custom_call_target="tpu_custom_call" | custom-call | flops 3400000000 | bytes 2000000 | tf_op jit(solution)/shard_map/pallas_call | solution.py:216
Async XLA Ops:
  0.0 0.7 copy-start.2
  0.7 1.0 %copy-start = (f32[80,1024]{1,0:T(8,128)S(1)}, f32[80,1024]{1,0:T(8,128)}, u32[]{:S(2)}) copy-start(f32[80,1024]{1,0:T(8,128)} %strain_ref.1) | copy-start | bytes 983044
  2.2 23.5 %copy-start.1 = (s32[128]{0:T(128)S(1)}, s32[128]{0:T(128)}, u32[]{:S(2)}) copy-start(s32[128]{0:T(128)} %plan_ref.3) | copy-start | bytes 1540
  45.8 23.9 %all-to-all-start.2 = ((bf16[32,80,128]{2,1,0:T(8,128)(2,1)}), bf16[32,80,128]{2,1,0:T(8,128)(2,1)S(1)}, u32[]{:S(2)}, u32[]{:S(2)}) async-start(bf16[32,80,128]{2,1,0:T(8,128)(2,1)} %get-tuple-element.10), calls=%async_computation.2 | async-start | bytes 1310720 | tf_op jit(solution)/shard_map/all_to_all | solution.py:215

commit v4 on v3

--- a/solution.py
+++ b/solution.py
@@ -22,7 +22,7 @@
 
 CHAN = ("z", "yh", "x")
 SEG = ("yl", "core")
-SCATTER = ("z", "x")
+SCATTER = ("x", "z")
 CROSS = ("yh", "yl", "core")
 
 F32 = jnp.float32
@@ -77,7 +77,7 @@
     ).astype(BF16)
     flag_rows = flags[0 : PIECE_ROWS - ROWS, :]
     for piece in range(PIECES):
-        q, h = piece // 4, piece % 4
+        h, q = piece // 8, piece % 8
         data = full[h * ROWS : (h + 1) * ROWS, q * 128 : (q + 1) * 128]
         pieces_ref[piece] = jnp.concatenate([data, flag_rows], axis=0).astype(BF16)
 
@@ -85,7 +85,7 @@
 def pick_kernel(plan_ref, got_ref, out_ref):
     for k in range(4):
         block = plan_ref[k]
-        holder = (block // 16) * 4 + block % 4
+        holder = (block % 4) * 8 + block // 16
         value = got_ref[holder]
         for y in range(4):
             out_ref[y * 4 + k] = value
@@ -111,13 +111,13 @@
     order[...] = (iota((4 * 128, 4 * 128), 1) == target).astype(F32).astype(BF16)
     for w in range(WINDOWS):
         for g in range(GROUPS):
-            own = own_ref[w, g * GROUP : (g + 1) * GROUP, :].astype(F32)
-            own = jnp.concatenate([own, jnp.zeros((GROUP, PAD - WIN), F32)], axis=1)
+            own = own_ref[w, g * GROUP : (g + 1) * GROUP, :]
+            own = jnp.concatenate([own, jnp.zeros((GROUP, PAD - WIN), BF16)], axis=1)
             for b in range(COARSE):
                 shift = (LAGS // 2 - FINE * b) % PAD
                 moved = own if shift == 0 else pltpu.roll(own, shift, 1)
                 first = g * 128 + b * GROUP
-                rhs[w, first : first + GROUP, :] = moved.astype(BF16)
+                rhs[w, first : first + GROUP, :] = moved
     lane = iota((128, GROUPS * 128), 1)
     channel = (lane // 128) * GROUP + lane % GROUP
     widen = (iota((128, GROUPS * 128), 0) == channel).astype(F32).astype(BF16)
@@ -129,17 +129,17 @@
     pairs = jnp.maximum(pairs, 1.0)
     source[:, :, WIN:] = jnp.zeros((WINDOWS, CH, PAD - WIN), F32)
     for piece in range(PIECES):
-        q, h = piece // 4, piece % 4
+        h, q = piece // 8, piece % 8
         value = got_ref[piece].astype(F32)
         for w in range(WINDOWS):
             source[w, h * ROWS : (h + 1) * ROWS, q * 128 : (q + 1) * 128] = value[
                 w * ROWS : (w + 1) * ROWS
             ]
     for w in range(WINDOWS):
-        block = source[w]
+        block = source[w].astype(BF16)
         for a in range(FINE):
             moved = block if a == 0 else pltpu.roll(block, a, 1)
-            lhs[w, a * CH : (a + 1) * CH, :] = moved.astype(BF16)
+            lhs[w, a * CH : (a + 1) * CH, :] = moved
     for w in range(WINDOWS):
         partial = lax.dot_general(
             lhs[w], rhs[w], (((1,), (1,)), ((), ())), preferred_element_type=F32

time: 74.5 us -> 72.9 us (0.979)
  the two profiles are of different devices: /device:TPU:1 before, /device:TPU:64 now
where the time goes in v4:
time: 72.9 us; the launch traced here: 72.6 us
  blocking collectives  47.1 us (65%)
  waiting for transfers between devices  12.6 us (17%)
  Pallas kernels  6.75 us (9%)
  starting transfers between devices  4.46 us (6%)
  local copies, waits for them, and re-layouts  1.63 us (2%)
    all_to_all x1, blocking collectives, per_device(): scattered = lax.all_to_all(pieces, SCATTER, 0, 0, tiled=True)  23.4 us
    all_to_all x1, blocking collectives, per_device(): crossed = lax.all_to_all(picked, CROSS, 0, 0, tiled=True)  15.3 us
    all_to_all x1, waiting for transfers between devices, per_device(): gathered = lax.all_to_all(fanned, SCATTER, 0, 0, tiled=True)  12.6 us
    all_gather x1, blocking collectives, per_device(): windows = lax.all_gather(own, SEG, axis=0)  8.39 us
    all_to_all x1, starting transfers between devices, per_device(): gathered = lax.all_to_all(fanned, SCATTER, 0, 0, tiled=True)  4.46 us
    pallas_call x1, Pallas kernels, per_device(): pl.pallas_call(correlate_kernel, out_shape=jax.ShapeDtypeStruct((CH, CH *...  4.15 us
    unnamed x6, local copies, waits for them, and re-layouts  1.63 us
  transfers between devices with their start and end apart: 1, of which 1 were waited for; matrix products, arithmetic and copies ran while one was open for 0% of the time, Pallas kernels for 0%

profile of v4, /device:TPU:64, one launch (start us, length us, event | category | flops | bytes accessed | tf_op | source)
XLA Modules:
  0.0 72.6 jit_solution(1252868570607377392)
XLA Ops:
  0.0 0.0 copy-start.2
  0.0 0.7 copy-done.2
  0.7 0.0 copy-start
  0.7 1.0 %copy-done = f32[80,1024]{1,0:T(8,128)S(1)} copy-done((f32[80,1024]{1,0:T(8,128)S(1)}, f32[80,1024]{1,0:T(8,128)}, u32[]{:S(2)}) %copy-start) | copy-done | bytes 327704
  1.6 0.6 shard_map.37
  2.2 0.0 copy-start.1
  2.2 23.4 %all_to_all.15.got_ref = bf16[32,24,128]{2,1,0:T(8,128)(2,1)S(1)} all-to-all(bf16[32,24,128]{2,1,0:T(8,128)(2,1)S(1)} %get-tuple-element.9), channel_id=1, replica_groups=mesh['z'=8,'yh'=4,'x'=4,'yl'=2,'core'=2] {'x','z'}, dimensions={0} | all-to-all | bytes 393216 | tf_op jit(solution)/shard_map/all_to_all | solution.py:195
  25.6 0.0 copy-done.1
  25.6 0.6 shard_map.38
  26.2 15.3 %all_to_all.16.got_ref = bf16[16,24,128]{2,1,0:T(8,128)(2,1)S(1)} all-to-all(bf16[16,24,128]{2,1,0:T(8,128)(2,1)S(1)} %shard_map.38), channel_id=1, replica_groups=mesh['z'=8,'yh'=4,'x'=4,'yl'=2,'core'=2] {'yh','yl','core'}, dimensions={0} | all-to-all | bytes 196608 | tf_op jit(solution)/shard_map/all_to_all | solution.py:204
  41.5 1.5 %shard_map.39 = (bf16[32,80,128]{2,1,0:T(8,128)(2,1)}, f32[8,128]{1,0:T(8,128)S(1)}) custom-call(s32[128]{0:T(128)S(1)} %copy-done.1, bf16[16,24,128]{2,1,0:T(8,128)(2,1)S(1)} %all_to_all.16.got_ref), custom_call_target="tpu_custom_call" | custom-call | tf_op jit(solution)/shard_map/pallas_call | solution.py:205
  43.0 4.5 %all-to-all-start.2 = ((bf16[32,80,128]{2,1,0:T(8,128)(2,1)}), bf16[32,80,128]{2,1,0:T(8,128)(2,1)S(1)}, u32[]{:S(2)}, u32[]{:S(2)}) async-start(bf16[32,80,128]{2,1,0:T(8,128)(2,1)} %get-tuple-element.10), calls=%async_computation.2 | async-start | bytes 1310720 | tf_op jit(solution)/shard_map/all_to_all | solution.py:215
  47.4 8.4 %all-gather = bf16[384,1024]{1,0:T(8,128)(2,1)S(1)} all-gather(bf16[96,1024]{1,0:T(8,128)(2,1)S(1)} %get-tuple-element.11), channel_id=2, replica_groups=mesh['z'=8,'yh'=4,'x'=4,'yl'=2,'core'=2] {'yl','core'}, dimensions={0}, use_global_device_ids=true | all-gather | bytes 983040 | tf_op jit(solution)/shard_map/all_gather | solution.py:196
  55.8 12.6 %all-to-all-done.2.got_ref = bf16[32,80,128]{2,1,0:T(8,128)(2,1)S(1)} async-done(((bf16[32,80,128]{2,1,0:T(8,128)(2,1)}), bf16[32,80,128]{2,1,0:T(8,128)(2,1)S(1)}, u32[]{:S(2)}, u32[]{:S(2)}) %all-to-all-start.2) | async-done | bytes 655392 | tf_op jit(solution)/shard_map/all_to_all | solution.py:215
  68.4 4.1 %shard_map.40 = bf16[80,2560]{1,0:T(8,128)(2,1)} custom-call(bf16[32,80,128]{2,1,0:T(8,128)(2,1)S(1)} %all-to-all-done.2.got_ref, bf16[4,96,1024]{2,1,0:T(8,128)(2,1)S(1)} %bitcast.2, f32[8,128]{1,0:T(8,128)S(1)} %get-tuple-element.12.flags_ref), custom_call_target="tpu_custom_call" | custom-call | flops 3400000000 | bytes 2000000 | tf_op jit(solution)/shard_map/pallas_call | solution.py:216
Async XLA Ops:
  0.0 0.7 copy-start.2
  0.7 1.0 %copy-start = (f32[80,1024]{1,0:T(8,128)S(1)}, f32[80,1024]{1,0:T(8,128)}, u32[]{:S(2)}) copy-start(f32[80,1024]{1,0:T(8,128)} %strain_ref.1) | copy-start | bytes 983044
  2.2 23.4 %copy-start.1 = (s32[128]{0:T(128)S(1)}, s32[128]{0:T(128)}, u32[]{:S(2)}) copy-start(s32[128]{0:T(128)} %plan_ref.3) | copy-start | bytes 1540
  43.0 25.5 %all-to-all-start.2 = ((bf16[32,80,128]{2,1,0:T(8,128)(2,1)}), bf16[32,80,128]{2,1,0:T(8,128)(2,1)S(1)}, u32[]{:S(2)}, u32[]{:S(2)}) async-start(bf16[32,80,128]{2,1,0:T(8,128)(2,1)} %get-tuple-element.10), calls=%async_computation.2 | async-start | bytes 1310720 | tf_op jit(solution)/shard_map/all_to_all | solution.py:215

commit v5 on v4

--- a/solution.py
+++ b/solution.py
@@ -23,7 +23,7 @@
 CHAN = ("z", "yh", "x")
 SEG = ("yl", "core")
 SCATTER = ("x", "z")
-CROSS = ("yh", "yl", "core")
+CROSS = ("core", "yh", "yl")
 
 F32 = jnp.float32
 BF16 = jnp.bfloat16
@@ -82,20 +82,24 @@
         pieces_ref[piece] = jnp.concatenate([data, flag_rows], axis=0).astype(BF16)
 
 
+def cross_slot(y, segment):
+    return (segment % 2) * 8 + y * 2 + segment // 2
+
+
 def pick_kernel(plan_ref, got_ref, out_ref):
     for k in range(4):
         block = plan_ref[k]
         holder = (block % 4) * 8 + block // 16
         value = got_ref[holder]
         for y in range(4):
-            out_ref[y * 4 + k] = value
+            out_ref[cross_slot(y, k)] = value
 
 
 def fan_kernel(plan_ref, got_ref, out_ref, flags_ref):
     pair = lax.axis_index("yl") * 2
     block = plan_ref[pair + lax.axis_index("core")]
     y = (block // 4) % 4
-    pieces = [got_ref[y * 4 + w].astype(F32) for w in range(WINDOWS)]
+    pieces = [got_ref[cross_slot(y, w)].astype(F32) for w in range(WINDOWS)]
     value = jnp.concatenate([p[:ROWS] for p in pieces], axis=0).astype(BF16)
     flag_rows = [p[ROWS : ROWS + 1] for p in pieces] + [jnp.zeros((4, 128), F32)]
     flags_ref[...] = jnp.concatenate(flag_rows, axis=0)

time: 72.9 us -> 72.3 us (level)
  the two profiles are of different devices: /device:TPU:64 before, /device:TPU:8 now
where the time goes in v5:
time: 72.3 us; the launch traced here: 72 us
  blocking collectives  47.2 us (65%)
  waiting for transfers between devices  12.3 us (17%)
  Pallas kernels  6.76 us (9%)
  starting transfers between devices  4.15 us (6%)
  local copies, waits for them, and re-layouts  1.63 us (2%)
    all_to_all x1, blocking collectives, per_device(): scattered = lax.all_to_all(pieces, SCATTER, 0, 0, tiled=True)  24.3 us
    all_to_all x1, blocking collectives, per_device(): crossed = lax.all_to_all(picked, CROSS, 0, 0, tiled=True)  14.9 us
    all_to_all x1, waiting for transfers between devices, per_device(): gathered = lax.all_to_all(fanned, SCATTER, 0, 0, tiled=True)  12.3 us
    all_gather x1, blocking collectives, per_device(): windows = lax.all_gather(own, SEG, axis=0)  7.98 us
    all_to_all x1, starting transfers between devices, per_device(): gathered = lax.all_to_all(fanned, SCATTER, 0, 0, tiled=True)  4.15 us
    pallas_call x1, Pallas kernels, per_device(): pl.pallas_call(correlate_kernel, out_shape=jax.ShapeDtypeStruct((CH, CH *...  4.15 us
    unnamed x6, local copies, waits for them, and re-layouts  1.63 us
    pallas_call x1, Pallas kernels, per_device(): pl.pallas_call(fan_kernel, out_shape=(jax.ShapeDtypeStruct((PIECES, SENT_...  1.45 us
  transfers between devices with their start and end apart: 1, of which 1 were waited for; matrix products, arithmetic and copies ran while one was open for 0% of the time, Pallas kernels for 0%

profile of v5, /device:TPU:8, one launch (start us, length us, event | category | flops | bytes accessed | tf_op | source)
XLA Modules:
  0.0 72.0 jit_solution(6646584880392908847)
XLA Ops:
  0.0 0.0 copy-start.2
  0.0 0.7 copy-done.2
  0.7 0.0 copy-start
  0.7 1.0 %copy-done = f32[80,1024]{1,0:T(8,128)S(1)} copy-done((f32[80,1024]{1,0:T(8,128)S(1)}, f32[80,1024]{1,0:T(8,128)}, u32[]{:S(2)}) %copy-start) | copy-done | bytes 327704
  1.6 0.6 shard_map.37
  2.2 0.0 copy-start.1
  2.2 24.3 %all_to_all.15.got_ref = bf16[32,24,128]{2,1,0:T(8,128)(2,1)S(1)} all-to-all(bf16[32,24,128]{2,1,0:T(8,128)(2,1)S(1)} %get-tuple-element.9), channel_id=1, replica_groups=mesh['z'=8,'yh'=4,'x'=4,'yl'=2,'core'=2] {'x','z'}, dimensions={0} | all-to-all | bytes 393216 | tf_op jit(solution)/shard_map/all_to_all | solution.py:199
  26.5 0.0 copy-done.1
  26.5 0.6 shard_map.38
  27.1 14.9 %all_to_all.16.got_ref = bf16[16,24,128]{2,1,0:T(8,128)(2,1)S(1)} all-to-all(bf16[16,24,128]{2,1,0:T(8,128)(2,1)S(1)} %shard_map.38), channel_id=1, replica_groups=mesh['z'=8,'yh'=4,'x'=4,'yl'=2,'core'=2] {'core','yh','yl'}, dimensions={0} | all-to-all | bytes 196608 | tf_op jit(solution)/shard_map/all_to_all | solution.py:208
  42.0 1.5 %shard_map.39 = (bf16[32,80,128]{2,1,0:T(8,128)(2,1)}, f32[8,128]{1,0:T(8,128)S(1)}) custom-call(s32[128]{0:T(128)S(1)} %copy-done.1, bf16[16,24,128]{2,1,0:T(8,128)(2,1)S(1)} %all_to_all.16.got_ref), custom_call_target="tpu_custom_call" | custom-call | tf_op jit(solution)/shard_map/pallas_call | solution.py:209
  43.5 4.2 %all-to-all-start.2 = ((bf16[32,80,128]{2,1,0:T(8,128)(2,1)}), bf16[32,80,128]{2,1,0:T(8,128)(2,1)S(1)}, u32[]{:S(2)}, u32[]{:S(2)}) async-start(bf16[32,80,128]{2,1,0:T(8,128)(2,1)} %get-tuple-element.10), calls=%async_computation.2 | async-start | bytes 1310720 | tf_op jit(solution)/shard_map/all_to_all | solution.py:219
  47.6 8.0 %all-gather = bf16[384,1024]{1,0:T(8,128)(2,1)S(1)} all-gather(bf16[96,1024]{1,0:T(8,128)(2,1)S(1)} %get-tuple-element.11), channel_id=2, replica_groups=mesh['z'=8,'yh'=4,'x'=4,'yl'=2,'core'=2] {'yl','core'}, dimensions={0}, use_global_device_ids=true | all-gather | bytes 983040 | tf_op jit(solution)/shard_map/all_gather | solution.py:200
  55.6 12.3 %all-to-all-done.2.got_ref = bf16[32,80,128]{2,1,0:T(8,128)(2,1)S(1)} async-done(((bf16[32,80,128]{2,1,0:T(8,128)(2,1)}), bf16[32,80,128]{2,1,0:T(8,128)(2,1)S(1)}, u32[]{:S(2)}, u32[]{:S(2)}) %all-to-all-start.2) | async-done | bytes 655392 | tf_op jit(solution)/shard_map/all_to_all | solution.py:219
  67.9 4.2 %shard_map.40 = bf16[80,2560]{1,0:T(8,128)(2,1)} custom-call(bf16[32,80,128]{2,1,0:T(8,128)(2,1)S(1)} %all-to-all-done.2.got_ref, bf16[4,96,1024]{2,1,0:T(8,128)(2,1)S(1)} %bitcast.2, f32[8,128]{1,0:T(8,128)S(1)} %get-tuple-element.12.flags_ref), custom_call_target="tpu_custom_call" | custom-call | flops 3400000000 | bytes 2000000 | tf_op jit(solution)/shard_map/pallas_call | solution.py:220
Async XLA Ops:
  0.0 0.7 copy-start.2
  0.7 1.0 %copy-start = (f32[80,1024]{1,0:T(8,128)S(1)}, f32[80,1024]{1,0:T(8,128)}, u32[]{:S(2)}) copy-start(f32[80,1024]{1,0:T(8,128)} %strain_ref.1) | copy-start | bytes 983044
  2.2 24.3 %copy-start.1 = (s32[128]{0:T(128)S(1)}, s32[128]{0:T(128)}, u32[]{:S(2)}) copy-start(s32[128]{0:T(128)} %plan_ref.3) | copy-start | bytes 1540
  43.5 24.4 %all-to-all-start.2 = ((bf16[32,80,128]{2,1,0:T(8,128)(2,1)}), bf16[32,80,128]{2,1,0:T(8,128)(2,1)S(1)}, u32[]{:S(2)}, u32[]{:S(2)}) async-start(bf16[32,80,128]{2,1,0:T(8,128)(2,1)} %get-tuple-element.10), calls=%async_computation.2 | async-start | bytes 1310720 | tf_op jit(solution)/shard_map/all_to_all | solution.py:219

commit v6 on v4

--- a/solution.py
+++ b/solution.py
@@ -20,10 +20,13 @@
 GROUP = 16
 GROUPS = CH // GROUP
 
-CHAN = ("z", "yh", "x")
+CHAN = ("z2", "z1", "z0", "y1", "y0", "x1", "x0")
 SEG = ("yl", "core")
-SCATTER = ("x", "z")
-CROSS = ("yh", "yl", "core")
+SCATTER = ('x1', 'x0', 'z2', 'z1', 'z0')
+GATHER = ('x1', 'x0', 'z1', 'z2', 'z0')
+CROSS = ('core', 'y1', 'y0', 'yl')
+
+PLACE = (0, 1, 4, 5, 2, 3, 6, 7, 8, 9, 12, 13, 10, 11, 14, 15, 16, 17, 20, 21, 18, 19, 22, 23, 24, 25, 28, 29, 26, 27, 30, 31)
 
 F32 = jnp.float32
 BF16 = jnp.bfloat16
@@ -77,7 +80,7 @@
     ).astype(BF16)
     flag_rows = flags[0 : PIECE_ROWS - ROWS, :]
     for piece in range(PIECES):
-        h, q = piece // 8, piece % 8
+        q, h = piece // 4, piece % 4
         data = full[h * ROWS : (h + 1) * ROWS, q * 128 : (q + 1) * 128]
         pieces_ref[piece] = jnp.concatenate([data, flag_rows], axis=0).astype(BF16)
 
@@ -85,17 +88,17 @@
 def pick_kernel(plan_ref, got_ref, out_ref):
     for k in range(4):
         block = plan_ref[k]
-        holder = (block % 4) * 8 + block // 16
+        holder = (block // 2 % 2) * 16 + (block % 2) * 8 + (block // 64 % 2) * 4 + (block // 32 % 2) * 2 + (block // 16 % 2)
         value = got_ref[holder]
         for y in range(4):
-            out_ref[y * 4 + k] = value
+            out_ref[4 * (y // 2) + 2 * (y % 2) + 1 * (k // 2) + 8 * (k % 2)] = value
 
 
 def fan_kernel(plan_ref, got_ref, out_ref, flags_ref):
     pair = lax.axis_index("yl") * 2
     block = plan_ref[pair + lax.axis_index("core")]
     y = (block // 4) % 4
-    pieces = [got_ref[y * 4 + w].astype(F32) for w in range(WINDOWS)]
+    pieces = [got_ref[4 * (y // 2) + 2 * (y % 2) + 1 * (w // 2) + 8 * (w % 2)].astype(F32) for w in range(WINDOWS)]
     value = jnp.concatenate([p[:ROWS] for p in pieces], axis=0).astype(BF16)
     flag_rows = [p[ROWS : ROWS + 1] for p in pieces] + [jnp.zeros((4, 128), F32)]
     flags_ref[...] = jnp.concatenate(flag_rows, axis=0)
@@ -129,7 +132,7 @@
     pairs = jnp.maximum(pairs, 1.0)
     source[:, :, WIN:] = jnp.zeros((WINDOWS, CH, PAD - WIN), F32)
     for piece in range(PIECES):
-        h, q = piece // 8, piece % 8
+        q, h = PLACE[piece] // 4, PLACE[piece] % 4
         value = got_ref[piece].astype(F32)
         for w in range(WINDOWS):
             source[w, h * ROWS : (h + 1) * ROWS, q * 128 : (q + 1) * 128] = value[
@@ -212,7 +215,7 @@
         out_specs=(vmem(), vmem()),
         compiler_params=params(),
     )(plan, crossed)
-    gathered = lax.all_to_all(fanned, SCATTER, 0, 0, tiled=True)
+    gathered = lax.all_to_all(fanned, GATHER, 0, 0, tiled=True)
     return pl.pallas_call(
         correlate_kernel,
         out_shape=jax.ShapeDtypeStruct((CH, CH * LAGS), BF16),
@@ -233,7 +236,7 @@
 
 
 def solution(mesh):
-    parts = Mesh(mesh.devices.reshape(8, 4, 4, 2, 2), ("z", "yh", "x", "yl", "core"))
+    parts = Mesh(mesh.devices.reshape((2,) * 9), CHAN + SEG)
     return jax.shard_map(
         per_device,
         mesh=parts,

time: 72.9 us -> 71.2 us (0.977)
  the two profiles are of different devices: /device:TPU:64 before, /device:TPU:8 now
where the time goes in v6:
time: 71.2 us; the launch traced here: 70.9 us
  blocking collectives  47.2 us (66%)
  waiting for transfers between devices  11.1 us (16%)
  Pallas kernels  6.83 us (10%)
  starting transfers between devices  4.15 us (6%)
  local copies, waits for them, and re-layouts  1.63 us (2%)
    all_to_all x1, blocking collectives, per_device(): scattered = lax.all_to_all(pieces, SCATTER, 0, 0, tiled=True)  24.3 us
    all_to_all x1, blocking collectives, per_device(): crossed = lax.all_to_all(picked, CROSS, 0, 0, tiled=True)  14.9 us
    all_to_all x1, waiting for transfers between devices, per_device(): gathered = lax.all_to_all(fanned, GATHER, 0, 0, tiled=True)  11.1 us
    all_gather x1, blocking collectives, per_device(): windows = lax.all_gather(own, SEG, axis=0)  7.98 us
    all_to_all x1, starting transfers between devices, per_device(): gathered = lax.all_to_all(fanned, GATHER, 0, 0, tiled=True)  4.15 us
    pallas_call x1, Pallas kernels, per_device(): pl.pallas_call(correlate_kernel, out_shape=jax.ShapeDtypeStruct((CH, CH *...  4.14 us
    unnamed x6, local copies, waits for them, and re-layouts  1.63 us
    pallas_call x1, Pallas kernels, per_device(): pl.pallas_call(fan_kernel, out_shape=(jax.ShapeDtypeStruct((PIECES, SENT_...  1.46 us
  transfers between devices with their start and end apart: 1, of which 1 were waited for; matrix products, arithmetic and copies ran while one was open for 0% of the time, Pallas kernels for 0%

profile of v6, /device:TPU:8, one launch (start us, length us, event | category | flops | bytes accessed | tf_op | source)
XLA Modules:
  0.0 70.9 jit_solution(10310792071827577102)
XLA Ops:
  0.0 0.0 copy-start.2
  0.0 0.7 copy-done.2
  0.7 0.0 copy-start
  0.7 1.0 %copy-done = f32[80,1024]{1,0:T(8,128)S(1)} copy-done((f32[80,1024]{1,0:T(8,128)S(1)}, f32[80,1024]{1,0:T(8,128)}, u32[]{:S(2)}) %copy-start) | copy-done | bytes 327704
  1.6 0.6 shard_map.37
  2.2 0.0 copy-start.1
  2.2 24.3 %all_to_all.15.got_ref = bf16[32,24,128]{2,1,0:T(8,128)(2,1)S(1)} all-to-all(bf16[32,24,128]{2,1,0:T(8,128)(2,1)S(1)} %get-tuple-element.9), channel_id=1, replica_groups=mesh['z2'=2,'z1'=2,'z0'=2,'y1'=2,'y0'=2,'x1'=2,'x0'=2,'yl'=2,'core'=2] {..., dimensions={0} | all-to-all | bytes 393216 | tf_op jit(solution)/shard_map/all_to_all | solution.py:198
  26.5 0.0 copy-done.1
  26.5 0.7 shard_map.38
  27.1 14.9 %all_to_all.16.got_ref = bf16[16,24,128]{2,1,0:T(8,128)(2,1)S(1)} all-to-all(bf16[16,24,128]{2,1,0:T(8,128)(2,1)S(1)} %shard_map.38), channel_id=1, replica_groups=mesh['z2'=2,'z1'=2,'z0'=2,'y1'=2,'y0'=2,'x1'=2,'x0'=2,'yl'=2,'core'=2] {..., dimensions={0} | all-to-all | bytes 196608 | tf_op jit(solution)/shard_map/all_to_all | solution.py:207
  42.1 1.5 %shard_map.39 = (bf16[32,80,128]{2,1,0:T(8,128)(2,1)}, f32[8,128]{1,0:T(8,128)S(1)}) custom-call(s32[128]{0:T(128)S(1)} %copy-done.1, bf16[16,24,128]{2,1,0:T(8,128)(2,1)S(1)} %all_to_all.16.got_ref), custom_call_target="tpu_custom_call" | custom-call | tf_op jit(solution)/shard_map/pallas_call | solution.py:208
  43.5 4.2 %all-to-all-start.2 = ((bf16[32,80,128]{2,1,0:T(8,128)(2,1)}), bf16[32,80,128]{2,1,0:T(8,128)(2,1)S(1)}, u32[]{:S(2)}, u32[]{:S(2)}) async-start(bf16[32,80,128]{2,1,0:T(8,128)(2,1)} %get-tuple-element.10), calls=%async_computation.2 | async-start | bytes 1310720 | tf_op jit(solution)/shard_map/all_to_all | solution.py:218
  47.7 8.0 %all-gather = bf16[384,1024]{1,0:T(8,128)(2,1)S(1)} all-gather(bf16[96,1024]{1,0:T(8,128)(2,1)S(1)} %get-tuple-element.11), channel_id=2, replica_groups=mesh['z2'=2,'z1'=2,'z0'=2,'y1'=2,'y0'=2,'x1'=2,'x0'=2,'yl'=2,'core'=2] {..., dimensions={0}, use_global_device_ids=true | all-gather | bytes 983040 | tf_op jit(solution)/shard_map/all_gather | solution.py:199
  55.7 11.1 %all-to-all-done.2.got_ref = bf16[32,80,128]{2,1,0:T(8,128)(2,1)S(1)} async-done(((bf16[32,80,128]{2,1,0:T(8,128)(2,1)}), bf16[32,80,128]{2,1,0:T(8,128)(2,1)S(1)}, u32[]{:S(2)}, u32[]{:S(2)}) %all-to-all-start.2) | async-done | bytes 655392 | tf_op jit(solution)/shard_map/all_to_all | solution.py:218
  66.8 4.1 %shard_map.40 = bf16[80,2560]{1,0:T(8,128)(2,1)} custom-call(bf16[32,80,128]{2,1,0:T(8,128)(2,1)S(1)} %all-to-all-done.2.got_ref, bf16[4,96,1024]{2,1,0:T(8,128)(2,1)S(1)} %bitcast.2, f32[8,128]{1,0:T(8,128)S(1)} %get-tuple-element.12.flags_ref), custom_call_target="tpu_custom_call" | custom-call | flops 3400000000 | bytes 2000000 | tf_op jit(solution)/shard_map/pallas_call | solution.py:219
Async XLA Ops:
  0.0 0.7 copy-start.2
  0.7 1.0 %copy-start = (f32[80,1024]{1,0:T(8,128)S(1)}, f32[80,1024]{1,0:T(8,128)}, u32[]{:S(2)}) copy-start(f32[80,1024]{1,0:T(8,128)} %strain_ref.1) | copy-start | bytes 983044
  2.2 24.3 %copy-start.1 = (s32[128]{0:T(128)S(1)}, s32[128]{0:T(128)}, u32[]{:S(2)}) copy-start(s32[128]{0:T(128)} %plan_ref.3) | copy-start | bytes 1540
  43.5 23.2 %all-to-all-start.2 = ((bf16[32,80,128]{2,1,0:T(8,128)(2,1)}), bf16[32,80,128]{2,1,0:T(8,128)(2,1)S(1)}, u32[]{:S(2)}, u32[]{:S(2)}) async-start(bf16[32,80,128]{2,1,0:T(8,128)(2,1)} %get-tuple-element.10), calls=%async_computation.2 | async-start | bytes 1310720 | tf_op jit(solution)/shard_map/all_to_all | solution.py:218

commit v7 on v6

--- a/solution.py
+++ b/solution.py
@@ -22,11 +22,9 @@
 
 CHAN = ("z2", "z1", "z0", "y1", "y0", "x1", "x0")
 SEG = ("yl", "core")
-SCATTER = ('x1', 'x0', 'z2', 'z1', 'z0')
+SCATTER = ('x1', 'x0', 'z1', 'z2', 'z0')
 GATHER = ('x1', 'x0', 'z1', 'z2', 'z0')
 CROSS = ('core', 'y1', 'y0', 'yl')
-
-PLACE = (0, 1, 4, 5, 2, 3, 6, 7, 8, 9, 12, 13, 10, 11, 14, 15, 16, 17, 20, 21, 18, 19, 22, 23, 24, 25, 28, 29, 26, 27, 30, 31)
 
 F32 = jnp.float32
 BF16 = jnp.bfloat16
@@ -88,7 +86,7 @@
 def pick_kernel(plan_ref, got_ref, out_ref):
     for k in range(4):
         block = plan_ref[k]
-        holder = (block // 2 % 2) * 16 + (block % 2) * 8 + (block // 64 % 2) * 4 + (block // 32 % 2) * 2 + (block // 16 % 2)
+        holder = (block // 2 % 2) * 16 + (block % 2) * 8 + (block // 32 % 2) * 4 + (block // 64 % 2) * 2 + (block // 16 % 2)
         value = got_ref[holder]
         for y in range(4):
             out_ref[4 * (y // 2) + 2 * (y % 2) + 1 * (k // 2) + 8 * (k % 2)] = value
@@ -132,7 +130,7 @@
     pairs = jnp.maximum(pairs, 1.0)
     source[:, :, WIN:] = jnp.zeros((WINDOWS, CH, PAD - WIN), F32)
     for piece in range(PIECES):
-        q, h = PLACE[piece] // 4, PLACE[piece] % 4
+        q, h = piece // 4, piece % 4
         value = got_ref[piece].astype(F32)
         for w in range(WINDOWS):
             source[w, h * ROWS : (h + 1) * ROWS, q * 128 : (q + 1) * 128] = value[

time: 71.2 us -> 71.2 us (level)
  no operation moved by 1% of the time
where the time goes in v7:
time: 71.2 us; the launch traced here: 70.9 us
  blocking collectives  46.6 us (65%)
  waiting for transfers between devices  11.1 us (16%)
  Pallas kernels  6.82 us (10%)
  starting transfers between devices  4.75 us (7%)
  local copies, waits for them, and re-layouts  1.63 us (2%)
    all_to_all x1, blocking collectives, per_device(): scattered = lax.all_to_all(pieces, SCATTER, 0, 0, tiled=True)  23.7 us
    all_to_all x1, blocking collectives, per_device(): crossed = lax.all_to_all(picked, CROSS, 0, 0, tiled=True)  14.9 us
    all_to_all x1, waiting for transfers between devices, per_device(): gathered = lax.all_to_all(fanned, GATHER, 0, 0, tiled=True)  11.1 us
    all_gather x1, blocking collectives, per_device(): windows = lax.all_gather(own, SEG, axis=0)  7.98 us
    all_to_all x1, starting transfers between devices, per_device(): gathered = lax.all_to_all(fanned, GATHER, 0, 0, tiled=True)  4.75 us
    pallas_call x1, Pallas kernels, per_device(): pl.pallas_call(correlate_kernel, out_shape=jax.ShapeDtypeStruct((CH, CH *...  4.14 us
    unnamed x6, local copies, waits for them, and re-layouts  1.63 us
    pallas_call x1, Pallas kernels, per_device(): pl.pallas_call(fan_kernel, out_shape=(jax.ShapeDtypeStruct((PIECES, SENT_...  1.46 us
  transfers between devices with their start and end apart: 1, of which 1 were waited for; matrix products, arithmetic and copies ran while one was open for 0% of the time, Pallas kernels for 0%

profile of v7, /device:TPU:8, one launch (start us, length us, event | category | flops | bytes accessed | tf_op | source)
XLA Modules:
  0.0 70.9 jit_solution(9348342297893533710)
XLA Ops:
  0.0 0.0 copy-start.2
  0.0 0.7 copy-done.2
  0.7 0.0 copy-start
  0.7 1.0 %copy-done = f32[80,1024]{1,0:T(8,128)S(1)} copy-done((f32[80,1024]{1,0:T(8,128)S(1)}, f32[80,1024]{1,0:T(8,128)}, u32[]{:S(2)}) %copy-start) | copy-done | bytes 327704
  1.6 0.6 shard_map.37
  2.2 0.0 copy-start.1
  2.2 23.7 %all_to_all.15.got_ref = bf16[32,24,128]{2,1,0:T(8,128)(2,1)S(1)} all-to-all(bf16[32,24,128]{2,1,0:T(8,128)(2,1)S(1)} %get-tuple-element.9), channel_id=1, replica_groups=mesh['z2'=2,'z1'=2,'z0'=2,'y1'=2,'y0'=2,'x1'=2,'x0'=2,'yl'=2,'core'=2] {..., dimensions={0} | all-to-all | bytes 393216 | tf_op jit(solution)/shard_map/all_to_all | solution.py:196
  25.9 0.0 copy-done.1
  25.9 0.7 shard_map.38
  26.5 14.9 %all_to_all.16.got_ref = bf16[16,24,128]{2,1,0:T(8,128)(2,1)S(1)} all-to-all(bf16[16,24,128]{2,1,0:T(8,128)(2,1)S(1)} %shard_map.38), channel_id=1, replica_groups=mesh['z2'=2,'z1'=2,'z0'=2,'y1'=2,'y0'=2,'x1'=2,'x0'=2,'yl'=2,'core'=2] {..., dimensions={0} | all-to-all | bytes 196608 | tf_op jit(solution)/shard_map/all_to_all | solution.py:205
  41.5 1.5 %shard_map.39 = (bf16[32,80,128]{2,1,0:T(8,128)(2,1)}, f32[8,128]{1,0:T(8,128)S(1)}) custom-call(s32[128]{0:T(128)S(1)} %copy-done.1, bf16[16,24,128]{2,1,0:T(8,128)(2,1)S(1)} %all_to_all.16.got_ref), custom_call_target="tpu_custom_call" | custom-call | tf_op jit(solution)/shard_map/pallas_call | solution.py:206
  42.9 4.7 %all-to-all-start.2 = ((bf16[32,80,128]{2,1,0:T(8,128)(2,1)}), bf16[32,80,128]{2,1,0:T(8,128)(2,1)S(1)}, u32[]{:S(2)}, u32[]{:S(2)}) async-start(bf16[32,80,128]{2,1,0:T(8,128)(2,1)} %get-tuple-element.10), calls=%async_computation.2 | async-start | bytes 1310720 | tf_op jit(solution)/shard_map/all_to_all | solution.py:216
  47.7 8.0 %all-gather = bf16[384,1024]{1,0:T(8,128)(2,1)S(1)} all-gather(bf16[96,1024]{1,0:T(8,128)(2,1)S(1)} %get-tuple-element.11), channel_id=2, replica_groups=mesh['z2'=2,'z1'=2,'z0'=2,'y1'=2,'y0'=2,'x1'=2,'x0'=2,'yl'=2,'core'=2] {..., dimensions={0}, use_global_device_ids=true | all-gather | bytes 983040 | tf_op jit(solution)/shard_map/all_gather | solution.py:197
  55.7 11.1 %all-to-all-done.2.got_ref = bf16[32,80,128]{2,1,0:T(8,128)(2,1)S(1)} async-done(((bf16[32,80,128]{2,1,0:T(8,128)(2,1)}), bf16[32,80,128]{2,1,0:T(8,128)(2,1)S(1)}, u32[]{:S(2)}, u32[]{:S(2)}) %all-to-all-start.2) | async-done | bytes 655392 | tf_op jit(solution)/shard_map/all_to_all | solution.py:216
  66.7 4.1 %shard_map.40 = bf16[80,2560]{1,0:T(8,128)(2,1)} custom-call(bf16[32,80,128]{2,1,0:T(8,128)(2,1)S(1)} %all-to-all-done.2.got_ref, bf16[4,96,1024]{2,1,0:T(8,128)(2,1)S(1)} %bitcast.2, f32[8,128]{1,0:T(8,128)S(1)} %get-tuple-element.12.flags_ref), custom_call_target="tpu_custom_call" | custom-call | flops 3400000000 | bytes 2000000 | tf_op jit(solution)/shard_map/pallas_call | solution.py:217
Async XLA Ops:
  0.0 0.7 copy-start.2
  0.7 1.0 %copy-start = (f32[80,1024]{1,0:T(8,128)S(1)}, f32[80,1024]{1,0:T(8,128)}, u32[]{:S(2)}) copy-start(f32[80,1024]{1,0:T(8,128)} %strain_ref.1) | copy-start | bytes 983044
  2.2 23.7 %copy-start.1 = (s32[128]{0:T(128)S(1)}, s32[128]{0:T(128)}, u32[]{:S(2)}) copy-start(s32[128]{0:T(128)} %plan_ref.3) | copy-start | bytes 1540
  42.9 23.8 %all-to-all-start.2 = ((bf16[32,80,128]{2,1,0:T(8,128)(2,1)}), bf16[32,80,128]{2,1,0:T(8,128)(2,1)S(1)}, u32[]{:S(2)}, u32[]{:S(2)}) async-start(bf16[32,80,128]{2,1,0:T(8,128)(2,1)} %get-tuple-element.10), calls=%async_computation.2 | async-start | bytes 1310720 | tf_op jit(solution)/shard_map/all_to_all | solution.py:216
